TPU v7x, 512 devices: a whole 4x4x16 slice. The times are simulated.
512 devices in a mesh: hist: 256 (over z, x, y_lo, core), orb: 2 (over y_hi).
Axes of the slice: x: 4, y: 4 (y_hi: 2, y_lo: 2; y = y_hi * 2 + y_lo), z: 16, core: 2. Of those that a mesh axis runs over, the one named last changes fastest.
Arguments:
- g_hist: bfloat16 [512, 64, 32768], P('hist', 'orb'), may hold values from -6 to 6
- sigma_hist: bfloat16 [2, 64, 32768], P(None, None, 'hist'), may hold values from -0.03125 to 0.03125
- diag_inv: float32 [512, 64, 64], P('hist'), may hold values from -0.75 to 0.75
- previous: float32 [2, 512, 64, 64], P(None, 'hist', 'orb'), may hold values from -6 to 6
- block_of_slot: int32 [256], replicated, may hold values from 0 to 255, each once
- front_pos: int32 [2], replicated, may hold values from 256 to 511
Outputs:
- g_row: float32 [2, 512, 64, 64], P(None, 'hist', 'orb')
- sigma_row: float32 [2, 512, 64, 64], P(None, 'hist', 'orb')
Inputs may be any that keep to these rules, and one draw needn't show every extreme that they name: `block_of_slot`: every block index appears once.
All inputs are finite; a program needn't handle non-finite values.
Results may differ from a plain program's by a relative error of at most 0.0003.
Values may be sent and summed in bfloat16 or wider, within the bound.
No kernel may reach another device: no remote copies, remote signals or barrier semaphores. Data moves between devices by JAX's collectives and lax.ppermute only.
A program may use at most 64 MiB of HBM per device.

v0:
```python
import jax
import jax.numpy as jnp
from jax import lax
from jax.sharding import Mesh
from jax.sharding import PartitionSpec as P

HIST = ("hist_0", "hist_1", "hist_2", "hist_3")
COUPLING = 0.5


def from_root(value, axes, root):
    value = jnp.where(lax.axis_index(axes) == root, value, jnp.zeros_like(value))
    for axis in axes:
        value = lax.psum(value, axis)
    return value


def from_everyone(value, axis):
    count = lax.axis_size(axis)
    return lax.all_to_all(
        jnp.broadcast_to(value[None], (count, *value.shape)), axis, 0, 0, tiled=True
    )


def joined_along(blocks, dim):
    blocks = jnp.moveaxis(blocks, 0, dim)
    lengths = blocks.shape
    return blocks.reshape(*lengths[:dim], lengths[dim] * lengths[dim + 1], *lengths[dim + 2 :])


def gathered_copies(value, axis, dim):
    blocks = from_everyone(value, axis)
    return joined_along(blocks, dim)


def contract(g_piece, s_piece, times, col_time, front_pos):
    g_kept = jnp.where(
        (times[None, :] >= col_time[:, None])[:, None, :], g_piece, jnp.zeros_like(g_piece)
    )
    s_kept = jnp.where(
        (times[None, :] <= front_pos[:, None])[:, None, :], s_piece, jnp.zeros_like(s_piece)
    )
    return jnp.einsum("tcx,fax->ftca", g_kept, s_kept, preferred_element_type=jnp.float32)


def inverse_row(diag_inv, when, col_count):
    local = lax.dynamic_index_in_dim(diag_inv, when % col_count, 0, keepdims=False)
    return from_root(local, HIST, when // col_count)


def body(g_hist, sigma_hist, diag_inv, previous, block_of_slot, front_pos):
    col_count = g_hist.shape[0]
    half_cols = g_hist.shape[1]
    orb_width = sigma_hist.shape[1]
    orb_id = lax.axis_index("orb")
    slot_id = lax.axis_index(HIST)
    my_block = lax.dynamic_index_in_dim(block_of_slot, slot_id, 0, keepdims=False)
    col_time = my_block * col_count + jnp.arange(col_count, dtype=jnp.int32)
    piece = lax.all_gather(sigma_hist, HIST, axis=2, tiled=True)
    count = piece.shape[2]
    times = jnp.arange(count, dtype=jnp.int32) // orb_width
    integral = contract(g_hist, piece, times, col_time, front_pos)
    combined = previous + integral
    rows = jnp.stack([inverse_row(diag_inv, front_pos[front], col_count) for front in range(2)])
    g_row = jnp.einsum("ftcb,fab->ftca", combined, rows, precision=lax.Precision.HIGHEST)
    whole = gathered_copies(g_row, "orb", 2)
    mirror = jnp.swapaxes(lax.dynamic_slice_in_dim(whole, orb_id * half_cols, half_cols, 3), 2, 3)
    sigma_row = COUPLING * g_row * g_row * mirror
    return (g_row, sigma_row)


def solution(mesh):
    split = Mesh(
        mesh.devices.reshape(16, 4, 2, 2, mesh.shape["orb"]),
        ("hist_0", "hist_1", "hist_2", "hist_3", "orb"),
    )
    in_specs = (
        P(HIST, "orb", None),
        P(None, None, HIST),
        P(HIST, None, None),
        P(None, HIST, "orb", None),
        P(),
        P(),
    )
    out_specs = (P(None, HIST, "orb", None), P(None, HIST, "orb", None))
    return jax.shard_map(body, mesh=split, in_specs=in_specs, out_specs=out_specs, check_vma=False)
```

profile of v0, /device:TPU:2, one launch (start us, length us, event | category | flops | bytes accessed | tf_op | source)
XLA Modules:
  0.0 462.0 jit_solution(15964508195874430775)
XLA Ops:
  7.2 0.0 all-gather.2.cloned.1.call-start
  7.2 0.7 all-gather.2.cloned.1.call-update
  7.9 1.3 fusion.28
  14.5 1.3 dynamic_slice.14
  16.4 0.8 select_bitcast_fusion.1
  17.2 62.1 %all-reduce = (f32[64,64]{1,0:T(8,128)S(1)}, f32[64,64]{1,0:T(8,128)S(1)}) all-reduce(f32[64,64]{1,0:T(8,128)S(1)} %get-tuple-element.13, f32[64,64]{1,0:T(8,128)S(1)} %get-tuple-element.12), channel_id=1, replica_groups=mesh['hist_0'=16,'hist_1'=4,'hist_2'=2,'hist_3'=2,'orb'=2] {'hist_0'}, use_global_device_ids=true, to_apply=%region_4.5 | all-reduce | flops 8192 | bytes 65536 | tf_op jit(solution)/shard_map/psum | solution.py:14
  79.3 14.6 %all-reduce.1 = (f32[64,64]{1,0:T(8,128)S(1)}, f32[64,64]{1,0:T(8,128)S(1)}) all-reduce(f32[64,64]{1,0:T(8,128)S(1)} %get-tuple-element.2, f32[64,64]{1,0:T(8,128)S(1)} %get-tuple-element.3), channel_id=1, replica_groups=mesh['hist_0'=16,'hist_1'=4,'hist_2'=2,'hist_3'=2,'orb'=2] {'hist_1'}, use_global_device_ids=true, to_apply=%region_5.6 | all-reduce | flops 8192 | bytes 65536 | tf_op jit(solution)/shard_map/psum | solution.py:14
  94.0 8.9 %all-reduce.3 = (f32[64,64]{1,0:T(8,128)S(1)}, f32[64,64]{1,0:T(8,128)S(1)}) all-reduce(f32[64,64]{1,0:T(8,128)S(1)} %get-tuple-element.4, f32[64,64]{1,0:T(8,128)S(1)} %get-tuple-element.5), channel_id=1, replica_groups=mesh['hist_0'=16,'hist_1'=4,'hist_2'=2,'hist_3'=2,'orb'=2] {'hist_2'}, use_global_device_ids=true, to_apply=%region_6.7 | all-reduce | flops 8192 | bytes 65536 | tf_op jit(solution)/shard_map/psum | solution.py:14
  102.9 3.6 all-reduce.2
  106.6 1.0 broadcast_compare_fusion.1
  107.6 325.5 %all-gather.2.cloned.1.call-done = bf16[2,64,32768]{2,1,0:T(8,128)(2,1)} async-done(((bf16[2,64,128]{2,1,0:T(8,128)(2,1)}), bf16[2,64,32768]{2,1,0:T(8,128)(2,1)}) %all-gather.2.cloned.1.call-update) | async-done | bytes 8388624 | tf_op jit(solution)/shard_map/all_gather | solution.py:59
  433.0 8.8 %fusion.14 = f32[2,2,32,64]{3,2,1,0:T(8,128)S(1)} fusion(f32[2,2,32,64]{3,2,1,0:T(8,128)} %param.9, bf16[2,32,32768]{2,1,0:T(8,128)(2,1)} %param.6, pred[2,32768]{1,0:T(4,128)(4,1)S(1)} %get-tuple-element.11, bf16[2,64,32768]{2,1,0:T(8,128)(2,1)} %all-gather.2.cloned.1.call-done, pred[2,32768]{1,0:T(4,128)(4,1)S(1)} %get-tuple-element.10), kind=kOutput, calls=%fused_computation.10 | convolution fusion | flops 543170560 | bytes 12779520 | tf_op jit(solution)/shard_map/tcx,fax->ftca/dot_general | solution.py:43
  441.8 0.2 fusion.23
  442.0 0.0 copy-start
  442.1 0.8 reshape.83
  442.8 4.3 all-to-all-start
  447.2 5.6 %all-to-all-done = f32[2,1,8192]{2,1,0:T(1,128)S(1)} async-done(((f32[2,1,8192]{2,1,0:T(1,128)}), f32[2,1,8192]{2,1,0:T(1,128)S(1)}, u32[]{:S(2)}, u32[]{:S(2)}) %all-to-all-start) | async-done | bytes 65568 | tf_op jit(solution)/shard_map/all_to_all | solution.py:20
  452.8 0.5 broadcast.82
  453.3 0.8 reduce
  454.1 0.1 reshape.84
  454.3 0.1 constant_dynamic-slice_fusion
  454.4 0.1 copy.14
  454.5 0.6 fusion.22
  455.1 0.0 copy-done
  (4 shorter events, 0.0 us)
Async XLA Ops:
  7.2 425.9 %all-gather.2.cloned.1.call-start = ((), (), s32[]{:S(2)}) async-start(), calls=%async_computation.1 | async-start | bytes 8421376 | tf_op jit(solution)/shard_map/all_gather | solution.py:59
  442.0 13.1 %copy-start = (f32[2,2,32,64]{3,2,1,0:T(8,128)}, f32[2,2,32,64]{3,2,1,0:T(8,128)S(1)}, u32[]{:S(2)}) copy-start(f32[2,2,32,64]{3,2,1,0:T(8,128)S(1)} %fusion.23) | copy-start | bytes 98308
  442.8 9.9 %all-to-all-start = ((f32[2,1,8192]{2,1,0:T(1,128)}), f32[2,1,8192]{2,1,0:T(1,128)S(1)}, u32[]{:S(2)}, u32[]{:S(2)}) async-start(f32[2,1,8192]{2,1,0:T(1,128)} %reshape.83), calls=%async_computation | async-start | bytes 131072 | tf_op jit(solution)/shard_map/all_to_all | solution.py:20
Sparse Core Ops, SparseCore 0:
  10.1 422.8 all-gather.1
where the time goes:
time: 462 us
  waiting for transfers between devices  332 us (72%)
  blocking collectives  89.3 us (19%)
  between operations  20 us (4%)
  matrix products  9 us (2%)
    all_gather x1, waiting for transfers between devices, body(): piece = lax.all_gather(sigma_hist, HIST, axis=2, tiled=True)  325 us
    psum x4, blocking collectives, from_root(): value = lax.psum(value, axis)  89.3 us
  transfers between devices with their start and end apart: 2, of which 2 were waited for; matrix products, arithmetic and copies ran while one was open for 1% of the time, Pallas kernels for 0%

commit v1 on v0

--- a/solution.py
+++ b/solution.py
@@ -56,7 +56,9 @@
     slot_id = lax.axis_index(HIST)
     my_block = lax.dynamic_index_in_dim(block_of_slot, slot_id, 0, keepdims=False)
     col_time = my_block * col_count + jnp.arange(col_count, dtype=jnp.int32)
-    piece = lax.all_gather(sigma_hist, HIST, axis=2, tiled=True)
+    piece = jnp.concatenate(
+        lax.all_to_all(jnp.stack([sigma_hist] * lax.axis_size(HIST)), HIST, 0, 0), axis=2
+    )
     count = piece.shape[2]
     times = jnp.arange(count, dtype=jnp.int32) // orb_width
     integral = contract(g_hist, piece, times, col_time, front_pos)

time: 462 us -> 490 us (1.061)
  the two profiles are of different devices: /device:TPU:2 before, /device:TPU:1 now
where the time goes in v1:
time: 490 us; the launch traced here: 489 us
  blocking collectives  433 us (88%)
  starting transfers between devices  27.9 us (6%)
  local copies, waits for them, and re-layouts  8.91 us (2%)
  between operations  6.69 us (1%)
  matrix products  6.42 us (1%)
    psum x4, blocking collectives, from_root(): value = lax.psum(value, axis)  433 us
    all_to_all x1, starting transfers between devices, body(): lax.all_to_all(jnp.stack([sigma_hist] * lax.axis_size(HIST)), HIST, 0, 0)  24.1 us
  transfers between devices with their start and end apart: 2, of which 1 were waited for; matrix products, arithmetic and copies ran while one was open for 0% of the time, Pallas kernels for 0%

profile of v1, /device:TPU:1, one launch (start us, length us, event | category | flops | bytes accessed | tf_op | source)
XLA Modules:
  0.0 489.5 jit_solution(6273568145058361111)
XLA Ops:
  0.6 6.1 %stack.8 = bf16[256,2,64,128]{3,2,1,0:T(8,128)(2,1)} broadcast(bf16[2,64,128]{2,1,0:T(8,128)(2,1)} %param.7), dimensions={1,2,3} | broadcast | bytes 8421376 | tf_op jit(solution)/shard_map/stack | solution.py:60
  6.7 0.0 copy-start.2
  6.7 0.0 copy-start.4
  6.7 0.0 copy-start.1
  6.7 0.0 copy-start.3
  6.8 24.1 %all-to-all-start = ((bf16[256,2,64,128]{3,2,1,0:T(8,128)(2,1)}), bf16[256,2,64,128]{3,2,1,0:T(8,128)(2,1)}, u32[]{:S(2)}, u32[]{:S(2)}) async-start(bf16[256,2,64,128]{3,2,1,0:T(8,128)(2,1)} %stack.8), calls=%async_computation | async-start | bytes 16777216 | tf_op jit(solution)/shard_map/all_to_all | solution.py:60
  30.8 0.0 copy-done.2
  30.8 0.6 fusion.29
  36.6 0.0 copy-done.4
  36.7 0.6 dynamic_slice.14
  37.9 0.0 copy-done.1
  37.9 390.4 %all-reduce = (f32[64,64]{1,0:T(8,128)S(1)}, f32[64,64]{1,0:T(8,128)S(1)}) all-reduce(f32[64,64]{1,0:T(8,128)S(1)} %get-tuple-element.13, f32[64,64]{1,0:T(8,128)S(1)} %get-tuple-element.12), channel_id=1, replica_groups=mesh['hist_0'=16,'hist_1'=4,'hist_2'=2,'hist_3'=2,'orb'=2] {'hist_0'}, use_global_device_ids=true, to_apply=%region_4.5 | all-reduce | flops 8192 | bytes 65536 | tf_op jit(solution)/shard_map/psum | solution.py:14
  428.3 13.3 %all-reduce.1 = (f32[64,64]{1,0:T(8,128)S(1)}, f32[64,64]{1,0:T(8,128)S(1)}) all-reduce(f32[64,64]{1,0:T(8,128)S(1)} %get-tuple-element.2, f32[64,64]{1,0:T(8,128)S(1)} %get-tuple-element.3), channel_id=1, replica_groups=mesh['hist_0'=16,'hist_1'=4,'hist_2'=2,'hist_3'=2,'orb'=2] {'hist_1'}, use_global_device_ids=true, to_apply=%region_5.6 | all-reduce | flops 8192 | bytes 65536 | tf_op jit(solution)/shard_map/psum | solution.py:14
  441.7 6.4 %all-reduce.3 = (f32[64,64]{1,0:T(8,128)S(1)}, f32[64,64]{1,0:T(8,128)S(1)}) all-reduce(f32[64,64]{1,0:T(8,128)S(1)} %get-tuple-element.4, f32[64,64]{1,0:T(8,128)S(1)} %get-tuple-element.5), channel_id=1, replica_groups=mesh['hist_0'=16,'hist_1'=4,'hist_2'=2,'hist_3'=2,'orb'=2] {'hist_2'}, use_global_device_ids=true, to_apply=%region_6.7 | all-reduce | flops 8192 | bytes 65536 | tf_op jit(solution)/shard_map/psum | solution.py:14
  448.0 23.1 %all-reduce.2 = (f32[1,64,64]{2,1,0:T(8,128)S(1)}, f32[1,64,64]{2,1,0:T(8,128)S(1)}) all-reduce(f32[1,64,64]{2,1,0:T(8,128)S(1)} %bitcast.55, f32[1,64,64]{2,1,0:T(8,128)S(1)} %bitcast.56), channel_id=1, replica_groups=mesh['hist_0'=16,'hist_1'=4,'hist_2'=2,'hist_3'=2,'orb'=2] {'hist_3'}, use_global_device_ids=true, to_apply=%region_7.8 | all-reduce | flops 8192 | bytes 65536 | tf_op jit(solution)/shard_map/psum | solution.py:14
  471.2 0.3 broadcast_compare_fusion.1
  471.5 0.0 all-to-all-done
  471.5 0.0 copy-done.3
  471.5 6.2 %fusion.15 = f32[2,2,32,64]{3,2,1,0:T(8,128)S(1)} fusion(f32[2,2,32,64]{3,2,1,0:T(8,128)S(1)} %copy-done.3, bf16[2,32,32768]{2,1,0:T(8,128)(2,1)} %param.6, pred[2,32768]{1,0:T(4,128)(4,1)S(1)} %get-tuple-element.11, pred[2,32768]{1,0:T(4,128)(4,1)S(1)} %get-tuple-element.10, bf16[256,2,64,128]{3,2,1,0:T(8,128)(2,1)} %all-to-all-done), kind=kOutput, calls=%fused_computation.11 | convolution fusion | flops 543170560 | bytes 12779520 | tf_op jit(solution)/shard_map/tcx,fax->ftca/dot_general | solution.py:43
  477.7 0.2 fusion.24
  478.0 0.0 copy-start
  478.0 0.8 reshape.93
  478.8 3.9 all-to-all-start.1
  482.6 4.5 all-to-all-done.1
  487.1 0.5 broadcast.84
  487.6 0.8 reduce
  488.5 0.1 reshape.94
  488.6 0.1 constant_dynamic-slice_fusion
  488.7 0.1 copy.17
  488.8 0.6 fusion.23
  489.5 0.0 copy-done
  (5 shorter events, 0.1 us)
Async XLA Ops:
  6.7 24.1 %copy-start.2 = (s32[2]{0:T(128)S(1)}, s32[2]{0:T(128)}, u32[]{:S(2)}) copy-start(s32[2]{0:T(128)} %param.11) | copy-start | bytes 28
  6.7 29.9 %copy-start.4 = (s32[256]{0:T(256)S(1)}, s32[256]{0:T(256)}, u32[]{:S(2)}) copy-start(s32[256]{0:T(256)} %param.10) | copy-start | bytes 3076
  6.7 31.2 %copy-start.1 = (f32[2,64,64]{2,1,0:T(8,128)S(1)}, f32[2,64,64]{2,1,0:T(8,128)}, u32[]{:S(2)}) copy-start(f32[2,64,64]{2,1,0:T(8,128)} %param.8) | copy-start | bytes 98308
  6.7 464.8 %copy-start.3 = (f32[2,2,32,64]{3,2,1,0:T(8,128)S(1)}, f32[2,2,32,64]{3,2,1,0:T(8,128)}, u32[]{:S(2)}) copy-start(f32[2,2,32,64]{3,2,1,0:T(8,128)} %param.9) | copy-start | bytes 98308
  6.8 464.8 %all-to-all-start = ((bf16[256,2,64,128]{3,2,1,0:T(8,128)(2,1)}), bf16[256,2,64,128]{3,2,1,0:T(8,128)(2,1)}, u32[]{:S(2)}, u32[]{:S(2)}) async-start(bf16[256,2,64,128]{3,2,1,0:T(8,128)(2,1)} %stack.8), calls=%async_computation | async-start | bytes 16777216 | tf_op jit(solution)/shard_map/all_to_all | solution.py:60
  478.0 11.5 %copy-start = (f32[2,2,32,64]{3,2,1,0:T(8,128)}, f32[2,2,32,64]{3,2,1,0:T(8,128)S(1)}, u32[]{:S(2)}) copy-start(f32[2,2,32,64]{3,2,1,0:T(8,128)S(1)} %fusion.24) | copy-start | bytes 98308
  478.8 8.4 %all-to-all-start.1 = ((f32[2,1,8192]{2,1,0:T(1,128)}), f32[2,1,8192]{2,1,0:T(1,128)S(1)}, u32[]{:S(2)}, u32[]{:S(2)}) async-start(f32[2,1,8192]{2,1,0:T(1,128)} %reshape.93), calls=%async_computation.1 | async-start | bytes 131072 | tf_op jit(solution)/shard_map/all_to_all | solution.py:20
